TPU v7x, 256 devices: a whole 4x4x8 slice. The times are simulated.
256 devices in a mesh: box: 64 (over x, z, core), cone: 4 (over y).
Axes of the slice: x: 4, y: 4, z: 8, core: 2. Of those that a mesh axis runs over, the one named last changes fastest.
Arguments:
- mom_current: bfloat16 [16384, 512], P('box'), may hold values from -6 to 6
- mom_radiate: bfloat16 [8, 512, 512], P('cone'), may hold values from -0.25 to 0.25
- po_receive: bfloat16 [8, 512, 512], P('cone'), may hold values from -0.09375 to 0.09375
- po_radiate: bfloat16 [8, 512, 512], P('cone'), may hold values from -0.25 to 0.25
- mom_receive: bfloat16 [8, 512, 512], P('cone'), may hold values from -0.03125 to 0.03125
- dirs: float32 [8, 3, 256], P('cone'), may hold values from -4 to 4
- mom_center: float32 [3, 16384], replicated, may hold values from 0 to 4
- po_center: float32 [3, 32768], replicated, may hold values from 0 to 4
- po_src: int32 [8, 32768], P(None, 'box'), may hold values from 0 to 16383, as said below
- po_weight: float32 [8, 32768], P(None, 'box'), may hold values from 0.2 to 2
- mom_src: int32 [8, 16384], P(None, 'box'), may hold values from 0 to 32767, as said below
- mom_weight: float32 [8, 16384], P(None, 'box'), may hold values from 0.2 to 2
- lit: int32 [8, 32768], P('cone', 'box'), may hold values 0 or 1
Outputs:
- mom_field: float32 [16384, 512], P('box', 'cone')
- po_current: bfloat16 [32768, 512], P('box', 'cone')
Inputs may be any that keep to these rules, and one draw needn't show every extreme that they name: |po_src[l, q] - q * 256 // 512| <= 256 for every entry. |mom_src[l, m] - m * 2| <= 512 for every entry.
All inputs are finite; a program needn't handle non-finite values. No bound on the sum of `lit` on one device may be relied on, other than what follows from the above.
Results may differ from a plain program's by a relative error of at most 0.0085.
Values may be sent and summed in bfloat16 or wider, within the bound.
No kernel may reach another device: no remote copies, remote signals or barrier semaphores. Data moves between devices by JAX's collectives and lax.ppermute only.
A program may use at most 64 MiB of HBM per device.

v0:
```python
import jax
import jax.numpy as jnp
from jax import lax
from jax.sharding import PartitionSpec as P


def padded_2(shard, sides, width):
    for axis, dim in sides:
        size, length = (lax.axis_size(axis), shard.shape[dim])
        up = [(i, (i + 1) % size) for i in range(size - 1)]
        down = [(j, i) for i, j in up]
        last = lax.slice_in_dim(shard, length - width, length, axis=dim)
        leading = lax.slice_in_dim(shard, 0, width, axis=dim)
        before = lax.ppermute(last, axis, up)
        after = lax.ppermute(leading, axis, down)
        shard = jnp.concatenate([before, shard, after], axis=dim)
    return shard


def phases(dirs, centers):
    return (
        centers[0][:, None, None] * dirs[None, :, 0, :]
        + centers[1][:, None, None] * dirs[None, :, 1, :]
        + centers[2][:, None, None] * dirs[None, :, 2, :]
    )


def rotate(waves, theta, orient):
    samples = theta.shape[-1]
    real_part = waves[..., :samples]
    imag_part = waves[..., samples:]
    cosine = jnp.cos(theta)
    sine = orient * jnp.sin(theta)
    return jnp.concatenate(
        [real_part * cosine - imag_part * sine, real_part * sine + imag_part * cosine], axis=-1
    )


def collect(padded, sources, weights, offset):
    rows_all, cone_count, width = padded.shape
    flat = padded.reshape(rows_all, cone_count * width)
    total = jnp.zeros((sources.shape[1], cone_count * width), jnp.float32)
    for slot in range(sources.shape[0]):
        picked = jnp.take(flat, sources[slot] - offset, axis=0).astype(jnp.float32)
        total = total + weights[slot][:, None] * picked
    return total.reshape(sources.shape[1], cone_count, width)


def shards(
    mom_current,
    mom_radiate,
    po_receive,
    po_radiate,
    mom_receive,
    dirs,
    mom_center,
    po_center,
    po_src,
    po_weight,
    mom_src,
    mom_weight,
    lit,
):
    box_index = lax.axis_index("box")
    mom_rows = mom_current.shape[0]
    po_rows = lit.shape[1]
    mom_theta = phases(
        dirs, lax.dynamic_slice_in_dim(mom_center, box_index * mom_rows, mom_rows, 1)
    )
    po_theta = phases(dirs, lax.dynamic_slice_in_dim(po_center, box_index * po_rows, po_rows, 1))
    radiated = jnp.einsum(
        "rn,cnk->rck", mom_current, mom_radiate, preferred_element_type=jnp.float32
    )
    mom_waves = rotate(radiated, mom_theta, -1.0).astype(jnp.bfloat16)
    mom_padded = padded_2(mom_waves, (("box", 0),), mom_rows)
    gathered = collect(mom_padded, po_src, po_weight, (box_index - 1) * mom_rows)
    lit_rows = jnp.transpose(lit).astype(jnp.float32)
    po_lit = (rotate(gathered, po_theta, 1.0) * lit_rows[:, :, None]).astype(jnp.bfloat16)
    partial_value = jnp.einsum(
        "rck,ckn->rn", po_lit, po_receive, preferred_element_type=jnp.float32
    )
    po_whole = lax.psum(partial_value, "cone").astype(jnp.bfloat16)
    share = po_whole.shape[1] // lax.axis_size("cone")
    po_share = lax.dynamic_slice_in_dim(po_whole, lax.axis_index("cone") * share, share, 1)
    radiated = jnp.einsum("rn,cnk->rck", po_whole, po_radiate, preferred_element_type=jnp.float32)
    po_waves = rotate(radiated, po_theta, -1.0).astype(jnp.bfloat16)
    po_padded = padded_2(po_waves, (("box", 0),), po_rows)
    returned = collect(po_padded, mom_src, mom_weight, (box_index - 1) * po_rows)
    mom_incident = rotate(returned, mom_theta, 1.0).astype(jnp.bfloat16)
    mom_partial = jnp.einsum(
        "rck,ckn->rn", mom_incident, mom_receive, preferred_element_type=jnp.float32
    )
    mom_field = lax.psum_scatter(mom_partial, "cone", scatter_dimension=1, tiled=True)
    return (mom_field, po_share)


def solution(mesh):
    in_specs = (
        P("box", None),
        P("cone", None, None),
        P("cone", None, None),
        P("cone", None, None),
        P("cone", None, None),
        P("cone", None, None),
        P(),
        P(),
        P(None, "box"),
        P(None, "box"),
        P(None, "box"),
        P(None, "box"),
        P("cone", "box"),
    )
    out_specs = (P("box", "cone"), P("box", "cone"))
    return jax.shard_map(shards, mesh=mesh, in_specs=in_specs, out_specs=out_specs, check_vma=False)
```

profile of v0, /device:TPU:2, one launch (start us, length us, event | category | flops | bytes accessed | tf_op | source)
XLA Modules:
  0.0 210.0 jit_solution(1306298672080685042)
XLA Ops:
  7.2 0.8 slice_bitcast_fusion.2
  8.0 1.8 fusion.14
  9.8 0.9 constant_dynamic-slice_fusion
  10.7 2.5 %subtract_convert_fusion.2 = (bf16[256,2,256]{2,0,1:T(8,128)(2,1)S(1)}, bf16[256,2,256]{2,0,1:T(8,128)(2,1)S(1)}) fusion(f32[256,2,512]{2,0,1:T(8,128)S(1)} %fusion.14, f32[2,256]{1,0:T(2,128)S(1)} %get-tuple-element.53, f32[256]{0:T(256)S(1)} %bitcast.110, f32[2,256]{1,0:T(2,128)S(1)} %get-tuple-element.54, f32[256]{0:T(256)S(1)} %bitcast.108, ...), kind=kLoop, calls=%fused_computation.43 | loop fusion | flops 1835008 | bytes 1582080 | tf_op jit(solution)/shard_map/convert.4
  13.3 1.9 collective-permute-start
  15.2 7.2 %collective-permute-start.1 = (bf16[256,2,512]{2,0,1:T(8,128)(2,1)S(1)}, bf16[256,2,512]{2,0,1:T(8,128)(2,1)}, u32[]{:S(2)}, u32[]{:S(2)}) collective-permute-start(bf16[256,2,512]{2,0,1:T(8,128)(2,1)S(1)} %pad_maximum_fusion.3), channel_id=1, source_target_pairs={{4,0},{8,4},{12,8},{16,12},{20,16},{24,20},{28,24},{32,28},{36,32}... | collective-permute-start | bytes 1572872 | tf_op jit(solution)/shard_map/ppermute | solution.py:15
  22.8 0.9 constant_dynamic-slice_fusion.2
  23.8 3.5 %collective-permute-done = bf16[256,2,512]{2,0,1:T(8,128)(2,1)S(1)} collective-permute-done((bf16[256,2,512]{2,0,1:T(8,128)(2,1)S(1)}, bf16[256,2,512]{2,0,1:T(8,128)(2,1)S(1)}, u32[]{:S(2)}, u32[]{:S(2)}) %collective-permute-start) | collective-permute-done | bytes 524320 | tf_op jit(solution)/shard_map/ppermute | solution.py:14
  27.3 0.8 copy-done.2
  28.1 1.0 collective-permute-done.1
  29.0 1.3 pad_maximum_fusion.1
  30.4 1.6 copy.26
  32.0 1.7 copy.27
  33.7 2.8 %gather_fusion = bf16[512,1024]{1,0:T(8,128)(2,1)} fusion(bf16[768,1024]{1,0:T(8,128)(2,1)S(1)} %copy.27, s32[1024]{0:T(1024)S(1)} %pad_clamp_fusion.15), kind=kCustom, calls=%fused_computation.clone | custom fusion | bytes 2099200 | tf_op jit(solution)/shard_map/jit(_take)/gather | solution.py:44
  36.5 2.8 %gather_fusion.1 = bf16[512,1024]{1,0:T(8,128)(2,1)} fusion(bf16[768,1024]{1,0:T(8,128)(2,1)S(1)} %copy.27, s32[1024]{0:T(1024)S(1)} %pad_clamp_fusion.14), kind=kCustom, calls=%fused_computation.2.clone | custom fusion | bytes 2099200 | tf_op jit(solution)/shard_map/jit(_take)/gather | solution.py:44
  39.3 2.8 %gather_fusion.2 = bf16[512,1024]{1,0:T(8,128)(2,1)} fusion(bf16[768,1024]{1,0:T(8,128)(2,1)S(1)} %copy.27, s32[1024]{0:T(1024)S(1)} %pad_clamp_fusion.13), kind=kCustom, calls=%fused_computation.3.clone | custom fusion | bytes 2099200 | tf_op jit(solution)/shard_map/jit(_take)/gather | solution.py:44
  42.1 2.8 %gather_fusion.3 = bf16[512,1024]{1,0:T(8,128)(2,1)} fusion(bf16[768,1024]{1,0:T(8,128)(2,1)S(1)} %copy.27, s32[1024]{0:T(1024)S(1)} %pad_clamp_fusion.12), kind=kCustom, calls=%fused_computation.4.clone | custom fusion | bytes 2099200 | tf_op jit(solution)/shard_map/jit(_take)/gather | solution.py:44
  44.9 2.8 %gather_fusion.4 = bf16[512,1024]{1,0:T(8,128)(2,1)} fusion(bf16[768,1024]{1,0:T(8,128)(2,1)S(1)} %copy.27, s32[1024]{0:T(1024)S(1)} %pad_clamp_fusion.11), kind=kCustom, calls=%fused_computation.5.clone | custom fusion | bytes 2099200 | tf_op jit(solution)/shard_map/jit(_take)/gather | solution.py:44
  47.6 2.8 %gather_fusion.5 = bf16[512,1024]{1,0:T(8,128)(2,1)} fusion(bf16[768,1024]{1,0:T(8,128)(2,1)S(1)} %copy.27, s32[1024]{0:T(1024)S(1)} %pad_clamp_fusion.10), kind=kCustom, calls=%fused_computation.6.clone | custom fusion | bytes 2099200 | tf_op jit(solution)/shard_map/jit(_take)/gather | solution.py:44
  50.4 2.8 %gather_fusion.6 = bf16[512,1024]{1,0:T(8,128)(2,1)} fusion(bf16[768,1024]{1,0:T(8,128)(2,1)S(1)} %copy.27, s32[1024]{0:T(1024)S(1)} %pad_clamp_fusion.9), kind=kCustom, calls=%fused_computation.7.clone | custom fusion | bytes 2099200 | tf_op jit(solution)/shard_map/jit(_take)/gather | solution.py:44
  53.1 2.8 %gather_fusion.7 = bf16[512,1024]{1,0:T(8,128)(2,1)} fusion(bf16[768,1024]{1,0:T(8,128)(2,1)S(1)} %copy.27, s32[1024]{0:T(1024)S(1)} %pad_clamp_fusion.8), kind=kCustom, calls=%fused_computation.8.clone | custom fusion | bytes 2099200 | tf_op jit(solution)/shard_map/jit(_take)/gather | solution.py:44
  55.9 5.2 %multiply_add_fusion = f32[512,1024]{1,0:T(8,128)S(1)} fusion(bf16[512,1024]{1,0:T(8,128)(2,1)} %gather_fusion.7, bf16[512,1024]{1,0:T(8,128)(2,1)} %gather_fusion.6, bf16[512,1024]{1,0:T(8,128)(2,1)} %gather_fusion.5, bf16[512,1024]{1,0:T(8,128)(2,1)} %gather_fusion.4, bf16[512,1024]{1,0:T(8,128)(2,1)} %gather_fusion.3, bf16[512,1024]{1,0:T(8,128)(2,1)} %gather_fusion.2, ...), kind=kLoop, calls=%fused_computation.19 | loop fusion | flops 16252928 | bytes 10506240 | tf_op jit(solution)/shard_map/add | solution.py:45
  61.1 1.8 copy.35
  63.0 7.1 %multiply_subtract_fusion = (f32[512,2,256]{0,2,1:T(8,128)S(1)}, f32[512,2,256]{0,2,1:T(8,128)S(1)}) fusion(f32[512,2,512]{0,2,1:T(8,128)} %bitcast.65, f32[2,256]{1,0:T(2,128)S(1)} %get-tuple-element.53, f32[512]{0:T(512)S(1)} %bitcast.72, f32[2,256]{1,0:T(2,128)S(1)} %get-tuple-element.54, f32[512]{0:T(512)S(1)} %bitcast.70, ...), kind=kLoop, calls=%fused_computation.29 | loop fusion | flops 2883584 | bytes 4206592 | tf_op jit(solution)/shard_map/sub | solution.py:35
  70.1 0.7 convolution_bitcast_fusion
  70.9 33.2 %all-reduce.1 = bf16[512,512]{1,0:T(8,128)(2,1)S(1)} all-reduce(f32[512,512]{1,0:T(8,128)S(1)} %convolution_bitcast_fusion), channel_id=1, replica_groups=mesh['box'=64,'cone'=4] {'cone'}, use_global_device_ids=true, to_apply=%region_0.0 | all-reduce | flops 262144 | bytes 1572864 | tf_op jit(solution)/shard_map/psum | solution.py:82
  104.1 0.8 fusion.9
  104.9 4.6 %subtract_convert_fusion = (bf16[512,2,256]{0,2,1:T(8,128)(2,1)S(1)}, bf16[512,2,256]{0,2,1:T(8,128)(2,1)S(1)}) fusion(f32[512,2,512]{0,2,1:T(8,128)S(1)} %fusion.9, f32[2,256]{1,0:T(2,128)S(1)} %get-tuple-element.53, f32[512]{0:T(512)S(1)} %bitcast.73, f32[2,256]{1,0:T(2,128)S(1)} %get-tuple-element.54, f32[512]{0:T(512)S(1)} %bitcast.71, ...), kind=kLoop, calls=%fused_computation.26 | loop fusion | flops 3670016 | bytes 3158016 | tf_op jit(solution)/shard_map/convert.2
  109.6 1.9 collective-permute-start.2
  111.5 5.8 %collective-permute-start.3 = (bf16[512,2,512]{0,2,1:T(8,128)(2,1)S(1)}, bf16[512,2,512]{0,2,1:T(8,128)(2,1)S(1)}, u32[]{:S(2)}, u32[]{:S(2)}) collective-permute-start(bf16[512,2,512]{0,2,1:T(8,128)(2,1)S(1)} %pad_maximum_fusion.2), channel_id=1, source_target_pairs={{4,0},{8,4},{12,8},{16,12},{20,16},{24,20},{28,24},{32,28},{36,32}... | collective-permute-start | bytes 3145736 | tf_op jit(solution)/shard_map/ppermute | solution.py:15
  117.4 10.4 %collective-permute-done.2 = bf16[512,2,512]{0,2,1:T(8,128)(2,1)S(1)} collective-permute-done((bf16[512,2,512]{0,2,1:T(8,128)(2,1)S(1)}, bf16[512,2,512]{0,2,1:T(8,128)(2,1)S(1)}, u32[]{:S(2)}, u32[]{:S(2)}) %collective-permute-start.2) | collective-permute-done | bytes 1048608 | tf_op jit(solution)/shard_map/ppermute | solution.py:14
  127.8 1.8 collective-permute-done.3
  129.6 1.8 pad_maximum_fusion
  131.4 4.7 %copy.38 = bf16[1536,1024]{1,0:T(8,128)(2,1)} copy(bf16[1536,1024]{0,1:T(8,128)(2,1)} %bitcast.64) | data formatting | bytes 6291456 | tf_op jit(solution)/shard_map/reshape | solution.py:41
  136.0 3.8 %gather_fusion.8 = bf16[256,1024]{1,0:T(8,128)(2,1)S(1)} fusion(bf16[1536,1024]{1,0:T(8,128)(2,1)} %copy.38, s32[1024]{0:T(1024)S(1)} %pad_clamp_fusion.7), kind=kCustom, calls=%fused_computation.1.clone | custom fusion | bytes 1049600 | tf_op jit(solution)/shard_map/jit(_take)/gather | solution.py:44
  139.9 3.9 %gather_fusion.9 = bf16[256,1024]{1,0:T(8,128)(2,1)S(1)} fusion(bf16[1536,1024]{1,0:T(8,128)(2,1)} %copy.38, s32[1024]{0:T(1024)S(1)} %pad_clamp_fusion.6), kind=kCustom, calls=%fused_computation.9.clone | custom fusion | bytes 1049600 | tf_op jit(solution)/shard_map/jit(_take)/gather | solution.py:44
  143.7 4.7 %gather_fusion.10 = bf16[256,1024]{1,0:T(8,128)(2,1)} fusion(bf16[1536,1024]{1,0:T(8,128)(2,1)} %copy.38, s32[1024]{0:T(1024)S(1)} %pad_clamp_fusion.5), kind=kCustom, calls=%fused_computation.10.clone | custom fusion | bytes 1049600 | tf_op jit(solution)/shard_map/jit(_take)/gather | solution.py:44
  148.4 4.6 %gather_fusion.11 = bf16[256,1024]{1,0:T(8,128)(2,1)} fusion(bf16[1536,1024]{1,0:T(8,128)(2,1)} %copy.38, s32[1024]{0:T(1024)S(1)} %pad_clamp_fusion.4), kind=kCustom, calls=%fused_computation.11.clone | custom fusion | bytes 1049600 | tf_op jit(solution)/shard_map/jit(_take)/gather | solution.py:44
  153.0 4.7 %gather_fusion.12 = bf16[256,1024]{1,0:T(8,128)(2,1)} fusion(bf16[1536,1024]{1,0:T(8,128)(2,1)} %copy.38, s32[1024]{0:T(1024)S(1)} %pad_clamp_fusion.3), kind=kCustom, calls=%fused_computation.12.clone | custom fusion | bytes 1049600 | tf_op jit(solution)/shard_map/jit(_take)/gather | solution.py:44
  157.7 4.7 %gather_fusion.13 = bf16[256,1024]{1,0:T(8,128)(2,1)} fusion(bf16[1536,1024]{1,0:T(8,128)(2,1)} %copy.38, s32[1024]{0:T(1024)S(1)} %pad_clamp_fusion.2), kind=kCustom, calls=%fused_computation.13.clone | custom fusion | bytes 1049600 | tf_op jit(solution)/shard_map/jit(_take)/gather | solution.py:44
  162.4 4.6 %gather_fusion.14 = bf16[256,1024]{1,0:T(8,128)(2,1)} fusion(bf16[1536,1024]{1,0:T(8,128)(2,1)} %copy.38, s32[1024]{0:T(1024)S(1)} %pad_clamp_fusion.1), kind=kCustom, calls=%fused_computation.14.clone | custom fusion | bytes 1049600 | tf_op jit(solution)/shard_map/jit(_take)/gather | solution.py:44
  167.0 4.6 %gather_fusion.15 = bf16[256,1024]{1,0:T(8,128)(2,1)} fusion(bf16[1536,1024]{1,0:T(8,128)(2,1)} %copy.38, s32[1024]{0:T(1024)S(1)} %pad_clamp_fusion), kind=kCustom, calls=%fused_computation.15.clone | custom fusion | bytes 1049600 | tf_op jit(solution)/shard_map/jit(_take)/gather | solution.py:44
  171.7 2.7 %multiply_add_fusion.1 = f32[256,1024]{1,0:T(8,128)S(1)} fusion(bf16[256,1024]{1,0:T(8,128)(2,1)} %gather_fusion.15, bf16[256,1024]{1,0:T(8,128)(2,1)} %gather_fusion.14, bf16[256,1024]{1,0:T(8,128)(2,1)} %gather_fusion.13, bf16[256,1024]{1,0:T(8,128)(2,1)} %gather_fusion.12, bf16[256,1024]{1,0:T(8,128)(2,1)} %gather_fusion.11, ...), kind=kLoop, calls=%fused_computation.24 | loop fusion | flops 8126464 | bytes 5253120 | tf_op jit(solution)/shard_map/add | solution.py:45
  174.4 0.3 copy.46
  175.2 2.5 %subtract_convert_fusion.1 = (bf16[256,2,256]{2,0,1:T(8,128)(2,1)S(1)}, bf16[256,2,256]{2,0,1:T(8,128)(2,1)S(1)}) fusion(f32[256,2,256]{2,0,1:T(8,128)S(1)} %copy.52, f32[256,2,256]{2,0,1:T(8,128)S(1)} %copy.51, f32[2,256]{1,0:T(2,128)S(1)} %get-tuple-element.53, f32[256]{0:T(256)S(1)} %bitcast.111, f32[2,256]{1,0:T(2,128)S(1)} %get-tuple-element.54, ...), kind=kLoop, calls=%fused_computation.41 | loop fusion | flops 1703936 | bytes 1582080 | tf_op jit(solution)/shard_map/convert
  177.8 2.5 %convolution_bitcast_fusion.1 = f32[256,512]{1,0:T(8,128)} fusion(bf16[2,512,512]{2,1,0:T(8,128)(2,1)} %param.21, bf16[256,2,256]{2,0,1:T(8,128)(2,1)S(1)} %get-tuple-element.9, bf16[256,2,256]{2,0,1:T(8,128)(2,1)S(1)} %get-tuple-element.8), kind=kOutput, calls=%fused_computation.22 | convolution fusion | flops 269484032 | bytes 2097152 | tf_op jit(solution)/shard_map/rck,ckn->rn/dot_general | solution.py:90
  180.2 1.6 constant_dynamic-slice_fusion.1
  181.8 21.3 %reduce-scatter.2.cloned.1.call-done = f32[256,128]{1,0:T(8,128)} async-done(((f32[256,512]{1,0:T(8,128)}), f32[256,128]{1,0:T(8,128)}) %reduce-scatter.2.cloned.1.call-update) | async-done | bytes 131088 | tf_op jit(solution)/shard_map/reduce_scatter | solution.py:93
  (65 shorter events, 1.0 us)
Async XLA Ops:
  7.2 97.0 %copy-start = (bf16[2,512,512]{2,1,0:T(8,128)(2,1)S(1)}, bf16[2,512,512]{2,1,0:T(8,128)(2,1)}, u32[]{:S(2)}) copy-start(bf16[2,512,512]{2,1,0:T(8,128)(2,1)} %param.20) | copy-start | bytes 3145732
  7.2 196.0 %reduce-scatter.2.cloned.1.call-start = ((), (), s32[]{:S(2)}) async-start(), calls=%async_computation.1 | async-start | bytes 655360 | tf_op jit(solution)/shard_map/reduce_scatter | solution.py:93
  8.0 14.3 %copy-start.3 = (s32[8,512]{1,0:T(8,128)S(1)}, s32[8,512]{1,0:T(8,128)}, u32[]{:S(2)}) copy-start(s32[8,512]{1,0:T(8,128)} %param.25) | copy-start | bytes 49156
  8.0 14.5 %copy-start.5 = (s32[8,256]{1,0:T(8,128)S(1)}, s32[8,256]{1,0:T(8,128)}, u32[]{:S(2)}) copy-start(s32[8,256]{1,0:T(8,128)} %param.27) | copy-start | bytes 24580
  8.0 15.7 %copy-start.7 = (s32[2,512]{1,0:T(2,128)S(1)}, s32[2,512]{1,0:T(2,128)}, u32[]{:S(2)}) copy-start(s32[2,512]{1,0:T(2,128)} %param.29) | copy-start | bytes 12292
  8.0 15.7 %copy-start.4 = (f32[8,512]{1,0:T(8,128)S(1)}, f32[8,512]{1,0:T(8,128)}, u32[]{:S(2)}) copy-start(f32[8,512]{1,0:T(8,128)} %param.26) | copy-start | bytes 49156
  13.3 14.0 %collective-permute-start = (bf16[256,2,512]{2,0,1:T(8,128)(2,1)S(1)}, bf16[256,2,512]{2,0,1:T(8,128)(2,1)S(1)}, u32[]{:S(2)}, u32[]{:S(2)}) collective-permute-start(bf16[256,2,512]{2,0,1:T(8,128)(2,1)S(1)} %pad_maximum_fusion.3), channel_id=1, source_target_pairs={{0,4},{4,8},{8,12},{12,16},{16,20},{20,24},{24,28},{28,32},{32,36}... | collective-permute-start | bytes 1572872 | tf_op jit(solution)/shard_map/ppermute | solution.py:14
  15.2 13.9 %collective-permute-start.1 = (bf16[256,2,512]{2,0,1:T(8,128)(2,1)S(1)}, bf16[256,2,512]{2,0,1:T(8,128)(2,1)}, u32[]{:S(2)}, u32[]{:S(2)}) collective-permute-start(bf16[256,2,512]{2,0,1:T(8,128)(2,1)S(1)} %pad_maximum_fusion.3), channel_id=1, source_target_pairs={{4,0},{8,4},{12,8},{16,12},{20,16},{24,20},{28,24},{32,28},{36,32}... | collective-permute-start | bytes 1572872 | tf_op jit(solution)/shard_map/ppermute | solution.py:15
  27.3 0.8 copy-start.2
  63.0 7.1 %copy-start.8 = (bf16[2,512,512]{2,1,0:T(8,128)(2,1)S(1)}, bf16[2,512,512]{2,1,0:T(8,128)(2,1)}, u32[]{:S(2)}) copy-start(bf16[2,512,512]{2,1,0:T(8,128)(2,1)} %param.19) | copy-start | bytes 3145732
  104.1 5.4 %copy-start.1 = (bf16[512,512]{1,0:T(8,128)(2,1)}, bf16[512,512]{1,0:T(8,128)(2,1)S(1)}, u32[]{:S(2)}) copy-start(bf16[512,512]{1,0:T(8,128)(2,1)S(1)} %all-reduce.1) | copy-start | bytes 1572868
  104.9 12.4 %copy-start.6 = (f32[8,256]{1,0:T(8,128)S(1)}, f32[8,256]{1,0:T(8,128)}, u32[]{:S(2)}) copy-start(f32[8,256]{1,0:T(8,128)} %param.28) | copy-start | bytes 24580
  109.6 18.2 %collective-permute-start.2 = (bf16[512,2,512]{0,2,1:T(8,128)(2,1)S(1)}, bf16[512,2,512]{0,2,1:T(8,128)(2,1)S(1)}, u32[]{:S(2)}, u32[]{:S(2)}) collective-permute-start(bf16[512,2,512]{0,2,1:T(8,128)(2,1)S(1)} %pad_maximum_fusion.2), channel_id=1, source_target_pairs={{0,4},{4,8},{8,12},{12,16},{16,20},{20,24},{24,28},{28,32},{32,36}... | collective-permute-start | bytes 3145736 | tf_op jit(solution)/shard_map/ppermute | solution.py:14
  111.5 18.1 %collective-permute-start.3 = (bf16[512,2,512]{0,2,1:T(8,128)(2,1)S(1)}, bf16[512,2,512]{0,2,1:T(8,128)(2,1)S(1)}, u32[]{:S(2)}, u32[]{:S(2)}) collective-permute-start(bf16[512,2,512]{0,2,1:T(8,128)(2,1)S(1)} %pad_maximum_fusion.2), channel_id=1, source_target_pairs={{4,0},{8,4},{12,8},{16,12},{20,16},{24,20},{28,24},{32,28},{36,32}... | collective-permute-start | bytes 3145736 | tf_op jit(solution)/shard_map/ppermute | solution.py:15
Sparse Core Ops, SparseCore 0:
  180.4 22.7 reduce-scatter.1
where the time goes:
time: 211 us; the launch traced here: 210 us
  local copies, waits for them, and re-layouts  73.5 us (35%)
  waiting for transfers between devices  38 us (18%)
  blocking collectives  33.2 us (16%)
  other arithmetic  28.1 us (13%)
  starting transfers between devices  16.8 us (8%)
  between operations  14.7 us (7%)
  matrix products  5.73 us (3%)
    gather x16, local copies, waits for them, and re-layouts, collect(): picked = jnp.take(flat, sources[slot] - offset, axis=0).astype(jnp.float32)  57.9 us
    psum x1, blocking collectives, shards(): po_whole = lax.psum(partial_value, 'cone').astype(jnp.bfloat16)  33.2 us
    reduce_scatter x1, waiting for transfers between devices, shards(): lax.psum_scatter(mom_partial, 'cone', scatter_dimension=1, tiled=True)  21.3 us
    ppermute x2, waiting for transfers between devices, padded_2(): before = lax.ppermute(last, axis, up)  13.9 us
    ppermute x2, starting transfers between devices, padded_2(): after = lax.ppermute(leading, axis, down)  12.9 us
    another operation x3, other arithmetic  9.56 us
    add x2, other arithmetic, collect(): total = total + weights[slot][:, None] * picked  7.95 us
    sub x1, other arithmetic, rotate(): real_part * cosine - imag_part * sine  7.12 us
  transfers between devices with their start and end apart: 5, of which 5 were waited for; matrix products, arithmetic and copies ran while one was open for 1% of the time, Pallas kernels for 0%

commit v1 on v0

--- a/solution.py
+++ b/solution.py
@@ -79,7 +79,8 @@
     partial_value = jnp.einsum(
         "rck,ckn->rn", po_lit, po_receive, preferred_element_type=jnp.float32
     )
-    po_whole = lax.psum(partial_value, "cone").astype(jnp.bfloat16)
+    _turn_skins = lambda xx: jnp.sum(lax.all_gather(xx, "cone"), 0)
+    po_whole = _turn_skins(partial_value).astype(jnp.bfloat16)
     share = po_whole.shape[1] // lax.axis_size("cone")
     po_share = lax.dynamic_slice_in_dim(po_whole, lax.axis_index("cone") * share, share, 1)
     radiated = jnp.einsum("rn,cnk->rck", po_whole, po_radiate, preferred_element_type=jnp.float32)

time: 211 us -> 235 us (1.11)
  waiting for transfers between devices: 38 us -> 91.1 us
  blocking collectives: 33.2 us -> 0 us
  other arithmetic: 28.1 us -> 30.8 us
    all_gather x0 -> x1, waiting for transfers between devices: none -> 51.8 us  [shards(): _turn_skins = lambda xx: jnp.sum(lax.all_gather(xx, 'cone'), 0)]
    psum x1 -> x0, blocking collectives: 33.2 us -> none  [shards(): po_whole = lax.psum(partial_value, 'cone').astype(jnp.bfloat16)]
    reduce_sum x0 -> x1, other arithmetic: none -> 2.73 us  [shards(): _turn_skins = lambda xx: jnp.sum(lax.all_gather(xx, 'cone'), 0)]
  transfers between devices with their start and end apart: 5 -> 6, of which waited for: 5 -> 6; matrix products, arithmetic and copies ran while one was open for 1% -> 1% of each run, Pallas kernels for 0% -> 0%
where the time goes in v1:
time: 235 us; the launch traced here: 234 us
  waiting for transfers between devices  91.1 us (39%)
  local copies, waits for them, and re-layouts  73.4 us (31%)
  other arithmetic  30.8 us (13%)
  starting transfers between devices  17 us (7%)
  between operations  14.7 us (6%)
  matrix products  6.75 us (3%)
    gather x16, local copies, waits for them, and re-layouts, collect(): picked = jnp.take(flat, sources[slot] - offset, axis=0).astype(jnp.float32)  57.8 us
    all_gather x1, waiting for transfers between devices, shards(): _turn_skins = lambda xx: jnp.sum(lax.all_gather(xx, 'cone'), 0)  51.8 us
    reduce_scatter x1, waiting for transfers between devices, shards(): lax.psum_scatter(mom_partial, 'cone', scatter_dimension=1, tiled=True)  22.5 us
    ppermute x2, waiting for transfers between devices, padded_2(): before = lax.ppermute(last, axis, up)  14.1 us
    ppermute x2, starting transfers between devices, padded_2(): after = lax.ppermute(leading, axis, down)  12.9 us
    another operation x3, other arithmetic  9.56 us
    add x2, other arithmetic, collect(): total = total + weights[slot][:, None] * picked  7.96 us
    sub x1, other arithmetic, rotate(): real_part * cosine - imag_part * sine  7.12 us
  transfers between devices with their start and end apart: 6, of which 6 were waited for; matrix products, arithmetic and copies ran while one was open for 1% of the time, Pallas kernels for 0%

profile of v1, /device:TPU:2, one launch (start us, length us, event | category | flops | bytes accessed | tf_op | source)
XLA Modules:
  0.0 233.8 jit_solution(3842827183392237135)
XLA Ops:
  7.2 0.8 slice_bitcast_fusion.2
  8.0 1.8 fusion.14
  9.8 0.9 constant_dynamic-slice_fusion
  10.7 2.5 %subtract_convert_fusion.2 = (bf16[256,2,256]{2,0,1:T(8,128)(2,1)S(1)}, bf16[256,2,256]{2,0,1:T(8,128)(2,1)S(1)}) fusion(f32[256,2,512]{2,0,1:T(8,128)S(1)} %fusion.14, f32[2,256]{1,0:T(2,128)S(1)} %get-tuple-element.53, f32[256]{0:T(256)S(1)} %bitcast.112, f32[2,256]{1,0:T(2,128)S(1)} %get-tuple-element.54, f32[256]{0:T(256)S(1)} %bitcast.110, ...), kind=kLoop, calls=%fused_computation.43 | loop fusion | flops 1835008 | bytes 1582080 | tf_op jit(solution)/shard_map/convert.4
  13.2 1.9 collective-permute-start
  15.2 7.2 %collective-permute-start.1 = (bf16[256,2,512]{2,0,1:T(8,128)(2,1)S(1)}, bf16[256,2,512]{2,0,1:T(8,128)(2,1)}, u32[]{:S(2)}, u32[]{:S(2)}) collective-permute-start(bf16[256,2,512]{2,0,1:T(8,128)(2,1)S(1)} %pad_maximum_fusion.3), channel_id=1, source_target_pairs={{4,0},{8,4},{12,8},{16,12},{20,16},{24,20},{28,24},{32,28},{36,32}... | collective-permute-start | bytes 1572872 | tf_op jit(solution)/shard_map/ppermute | solution.py:15
  22.6 0.9 constant_dynamic-slice_fusion.2
  23.6 3.7 %collective-permute-done = bf16[256,2,512]{2,0,1:T(8,128)(2,1)S(1)} collective-permute-done((bf16[256,2,512]{2,0,1:T(8,128)(2,1)S(1)}, bf16[256,2,512]{2,0,1:T(8,128)(2,1)S(1)}, u32[]{:S(2)}, u32[]{:S(2)}) %collective-permute-start) | collective-permute-done | bytes 524320 | tf_op jit(solution)/shard_map/ppermute | solution.py:14
  27.3 0.8 copy-done.2
  28.1 1.0 collective-permute-done.1
  29.0 1.3 pad_maximum_fusion.1
  30.3 1.6 copy.26
  31.9 1.7 copy.27
  33.7 2.8 %gather_fusion = bf16[512,1024]{1,0:T(8,128)(2,1)} fusion(bf16[768,1024]{1,0:T(8,128)(2,1)S(1)} %copy.27, s32[1024]{0:T(1024)S(1)} %pad_clamp_fusion.15), kind=kCustom, calls=%fused_computation.clone | custom fusion | bytes 2099200 | tf_op jit(solution)/shard_map/jit(_take)/gather | solution.py:44
  36.5 2.7 %gather_fusion.1 = bf16[512,1024]{1,0:T(8,128)(2,1)} fusion(bf16[768,1024]{1,0:T(8,128)(2,1)S(1)} %copy.27, s32[1024]{0:T(1024)S(1)} %pad_clamp_fusion.14), kind=kCustom, calls=%fused_computation.2.clone | custom fusion | bytes 2099200 | tf_op jit(solution)/shard_map/jit(_take)/gather | solution.py:44
  39.2 2.8 %gather_fusion.2 = bf16[512,1024]{1,0:T(8,128)(2,1)} fusion(bf16[768,1024]{1,0:T(8,128)(2,1)S(1)} %copy.27, s32[1024]{0:T(1024)S(1)} %pad_clamp_fusion.13), kind=kCustom, calls=%fused_computation.3.clone | custom fusion | bytes 2099200 | tf_op jit(solution)/shard_map/jit(_take)/gather | solution.py:44
  42.0 2.8 %gather_fusion.3 = bf16[512,1024]{1,0:T(8,128)(2,1)} fusion(bf16[768,1024]{1,0:T(8,128)(2,1)S(1)} %copy.27, s32[1024]{0:T(1024)S(1)} %pad_clamp_fusion.12), kind=kCustom, calls=%fused_computation.4.clone | custom fusion | bytes 2099200 | tf_op jit(solution)/shard_map/jit(_take)/gather | solution.py:44
  44.8 2.8 %gather_fusion.4 = bf16[512,1024]{1,0:T(8,128)(2,1)} fusion(bf16[768,1024]{1,0:T(8,128)(2,1)S(1)} %copy.27, s32[1024]{0:T(1024)S(1)} %pad_clamp_fusion.11), kind=kCustom, calls=%fused_computation.5.clone | custom fusion | bytes 2099200 | tf_op jit(solution)/shard_map/jit(_take)/gather | solution.py:44
  47.6 2.8 %gather_fusion.5 = bf16[512,1024]{1,0:T(8,128)(2,1)} fusion(bf16[768,1024]{1,0:T(8,128)(2,1)S(1)} %copy.27, s32[1024]{0:T(1024)S(1)} %pad_clamp_fusion.10), kind=kCustom, calls=%fused_computation.6.clone | custom fusion | bytes 2099200 | tf_op jit(solution)/shard_map/jit(_take)/gather | solution.py:44
  50.3 2.8 %gather_fusion.6 = bf16[512,1024]{1,0:T(8,128)(2,1)} fusion(bf16[768,1024]{1,0:T(8,128)(2,1)S(1)} %copy.27, s32[1024]{0:T(1024)S(1)} %pad_clamp_fusion.9), kind=kCustom, calls=%fused_computation.7.clone | custom fusion | bytes 2099200 | tf_op jit(solution)/shard_map/jit(_take)/gather | solution.py:44
  53.1 2.8 %gather_fusion.7 = bf16[512,1024]{1,0:T(8,128)(2,1)} fusion(bf16[768,1024]{1,0:T(8,128)(2,1)S(1)} %copy.27, s32[1024]{0:T(1024)S(1)} %pad_clamp_fusion.8), kind=kCustom, calls=%fused_computation.8.clone | custom fusion | bytes 2099200 | tf_op jit(solution)/shard_map/jit(_take)/gather | solution.py:44
  55.9 5.2 %multiply_add_fusion = f32[512,1024]{1,0:T(8,128)S(1)} fusion(bf16[512,1024]{1,0:T(8,128)(2,1)} %gather_fusion.7, bf16[512,1024]{1,0:T(8,128)(2,1)} %gather_fusion.6, bf16[512,1024]{1,0:T(8,128)(2,1)} %gather_fusion.5, bf16[512,1024]{1,0:T(8,128)(2,1)} %gather_fusion.4, bf16[512,1024]{1,0:T(8,128)(2,1)} %gather_fusion.3, bf16[512,1024]{1,0:T(8,128)(2,1)} %gather_fusion.2, ...), kind=kLoop, calls=%fused_computation.19 | loop fusion | flops 16252928 | bytes 10506240 | tf_op jit(solution)/shard_map/add | solution.py:45
  61.1 1.9 copy.35
  63.0 7.1 %multiply_subtract_fusion = (f32[512,2,256]{0,2,1:T(8,128)S(1)}, f32[512,2,256]{0,2,1:T(8,128)S(1)}) fusion(f32[512,2,512]{0,2,1:T(8,128)} %bitcast.66, f32[2,256]{1,0:T(2,128)S(1)} %get-tuple-element.53, f32[512]{0:T(512)S(1)} %bitcast.74, f32[2,256]{1,0:T(2,128)S(1)} %get-tuple-element.54, f32[512]{0:T(512)S(1)} %bitcast.72, ...), kind=kLoop, calls=%fused_computation.29 | loop fusion | flops 2883584 | bytes 4206592 | tf_op jit(solution)/shard_map/sub | solution.py:35
  70.1 1.8 convolution_bitcast_fusion
  72.3 51.8 %all-gather.3.cloned.1.call-done = f32[2048,512]{1,0:T(8,128)} async-done(((f32[512,512]{1,0:T(8,128)}), f32[2048,512]{1,0:T(8,128)}) %all-gather.3.cloned.1.call-update) | async-done | bytes 4194320 | tf_op jit(solution)/shard_map/all_gather | solution.py:82
  124.1 2.7 %reduce_sum.9 = bf16[512,512]{1,0:T(8,128)(2,1)S(1)} reduce(f32[4,512,512]{2,1,0:T(8,128)} %bitcast.68, f32[]{:T(128)} %constant.17.clone.1), dimensions={0}, to_apply=%region_0.0 | reduce | flops 786432 | bytes 4718596 | tf_op jit(solution)/shard_map/reduce_sum | solution.py:82
  126.9 0.8 fusion.9
  127.6 4.6 %subtract_convert_fusion = (bf16[512,2,256]{0,2,1:T(8,128)(2,1)S(1)}, bf16[512,2,256]{0,2,1:T(8,128)(2,1)S(1)}) fusion(f32[512,2,512]{0,2,1:T(8,128)S(1)} %fusion.9, f32[2,256]{1,0:T(2,128)S(1)} %get-tuple-element.53, f32[512]{0:T(512)S(1)} %bitcast.75, f32[2,256]{1,0:T(2,128)S(1)} %get-tuple-element.54, f32[512]{0:T(512)S(1)} %bitcast.73, ...), kind=kLoop, calls=%fused_computation.26 | loop fusion | flops 3670016 | bytes 3158016 | tf_op jit(solution)/shard_map/convert.2
  132.3 1.9 collective-permute-start.2
  134.2 5.8 %collective-permute-start.3 = (bf16[512,2,512]{0,2,1:T(8,128)(2,1)S(1)}, bf16[512,2,512]{0,2,1:T(8,128)(2,1)S(1)}, u32[]{:S(2)}, u32[]{:S(2)}) collective-permute-start(bf16[512,2,512]{0,2,1:T(8,128)(2,1)S(1)} %pad_maximum_fusion.2), channel_id=1, source_target_pairs={{4,0},{8,4},{12,8},{16,12},{20,16},{24,20},{28,24},{32,28},{36,32}... | collective-permute-start | bytes 3145736 | tf_op jit(solution)/shard_map/ppermute | solution.py:15
  140.1 10.4 %collective-permute-done.2 = bf16[512,2,512]{0,2,1:T(8,128)(2,1)S(1)} collective-permute-done((bf16[512,2,512]{0,2,1:T(8,128)(2,1)S(1)}, bf16[512,2,512]{0,2,1:T(8,128)(2,1)S(1)}, u32[]{:S(2)}, u32[]{:S(2)}) %collective-permute-start.2) | collective-permute-done | bytes 1048608 | tf_op jit(solution)/shard_map/ppermute | solution.py:14
  150.5 1.8 collective-permute-done.3
  152.3 1.8 pad_maximum_fusion
  154.1 4.6 %copy.38 = bf16[1536,1024]{1,0:T(8,128)(2,1)} copy(bf16[1536,1024]{0,1:T(8,128)(2,1)} %bitcast.65) | data formatting | bytes 6291456 | tf_op jit(solution)/shard_map/reshape | solution.py:41
  158.7 3.8 %gather_fusion.8 = bf16[256,1024]{1,0:T(8,128)(2,1)S(1)} fusion(bf16[1536,1024]{1,0:T(8,128)(2,1)} %copy.38, s32[1024]{0:T(1024)S(1)} %pad_clamp_fusion.7), kind=kCustom, calls=%fused_computation.1.clone | custom fusion | bytes 1049600 | tf_op jit(solution)/shard_map/jit(_take)/gather | solution.py:44
  162.6 3.9 %gather_fusion.9 = bf16[256,1024]{1,0:T(8,128)(2,1)S(1)} fusion(bf16[1536,1024]{1,0:T(8,128)(2,1)} %copy.38, s32[1024]{0:T(1024)S(1)} %pad_clamp_fusion.6), kind=kCustom, calls=%fused_computation.9.clone | custom fusion | bytes 1049600 | tf_op jit(solution)/shard_map/jit(_take)/gather | solution.py:44
  166.4 4.7 %gather_fusion.10 = bf16[256,1024]{1,0:T(8,128)(2,1)} fusion(bf16[1536,1024]{1,0:T(8,128)(2,1)} %copy.38, s32[1024]{0:T(1024)S(1)} %pad_clamp_fusion.5), kind=kCustom, calls=%fused_computation.10.clone | custom fusion | bytes 1049600 | tf_op jit(solution)/shard_map/jit(_take)/gather | solution.py:44
  171.1 4.6 %gather_fusion.11 = bf16[256,1024]{1,0:T(8,128)(2,1)} fusion(bf16[1536,1024]{1,0:T(8,128)(2,1)} %copy.38, s32[1024]{0:T(1024)S(1)} %pad_clamp_fusion.4), kind=kCustom, calls=%fused_computation.11.clone | custom fusion | bytes 1049600 | tf_op jit(solution)/shard_map/jit(_take)/gather | solution.py:44
  175.7 4.7 %gather_fusion.12 = bf16[256,1024]{1,0:T(8,128)(2,1)} fusion(bf16[1536,1024]{1,0:T(8,128)(2,1)} %copy.38, s32[1024]{0:T(1024)S(1)} %pad_clamp_fusion.3), kind=kCustom, calls=%fused_computation.12.clone | custom fusion | bytes 1049600 | tf_op jit(solution)/shard_map/jit(_take)/gather | solution.py:44
  180.4 4.7 %gather_fusion.13 = bf16[256,1024]{1,0:T(8,128)(2,1)} fusion(bf16[1536,1024]{1,0:T(8,128)(2,1)} %copy.38, s32[1024]{0:T(1024)S(1)} %pad_clamp_fusion.2), kind=kCustom, calls=%fused_computation.13.clone | custom fusion | bytes 1049600 | tf_op jit(solution)/shard_map/jit(_take)/gather | solution.py:44
  185.0 4.7 %gather_fusion.14 = bf16[256,1024]{1,0:T(8,128)(2,1)} fusion(bf16[1536,1024]{1,0:T(8,128)(2,1)} %copy.38, s32[1024]{0:T(1024)S(1)} %pad_clamp_fusion.1), kind=kCustom, calls=%fused_computation.14.clone | custom fusion | bytes 1049600 | tf_op jit(solution)/shard_map/jit(_take)/gather | solution.py:44
  189.7 4.6 %gather_fusion.15 = bf16[256,1024]{1,0:T(8,128)(2,1)} fusion(bf16[1536,1024]{1,0:T(8,128)(2,1)} %copy.38, s32[1024]{0:T(1024)S(1)} %pad_clamp_fusion), kind=kCustom, calls=%fused_computation.15.clone | custom fusion | bytes 1049600 | tf_op jit(solution)/shard_map/jit(_take)/gather | solution.py:44
  194.4 2.7 %multiply_add_fusion.1 = f32[256,1024]{1,0:T(8,128)S(1)} fusion(bf16[256,1024]{1,0:T(8,128)(2,1)} %gather_fusion.15, bf16[256,1024]{1,0:T(8,128)(2,1)} %gather_fusion.14, bf16[256,1024]{1,0:T(8,128)(2,1)} %gather_fusion.13, bf16[256,1024]{1,0:T(8,128)(2,1)} %gather_fusion.12, bf16[256,1024]{1,0:T(8,128)(2,1)} %gather_fusion.11, ...), kind=kLoop, calls=%fused_computation.24 | loop fusion | flops 8126464 | bytes 5253120 | tf_op jit(solution)/shard_map/add | solution.py:45
  197.9 2.5 %subtract_convert_fusion.1 = (bf16[256,2,256]{2,0,1:T(8,128)(2,1)S(1)}, bf16[256,2,256]{2,0,1:T(8,128)(2,1)S(1)}) fusion(f32[256,2,256]{2,0,1:T(8,128)S(1)} %copy.52, f32[256,2,256]{2,0,1:T(8,128)S(1)} %copy.51, f32[2,256]{1,0:T(2,128)S(1)} %get-tuple-element.53, f32[256]{0:T(256)S(1)} %bitcast.113, f32[2,256]{1,0:T(2,128)S(1)} %get-tuple-element.54, ...), kind=kLoop, calls=%fused_computation.41 | loop fusion | flops 1703936 | bytes 1582080 | tf_op jit(solution)/shard_map/convert
  200.4 2.5 %convolution_bitcast_fusion.1 = f32[256,512]{1,0:T(8,128)} fusion(bf16[2,512,512]{2,1,0:T(8,128)(2,1)} %param.21, bf16[256,2,256]{2,0,1:T(8,128)(2,1)S(1)} %get-tuple-element.9, bf16[256,2,256]{2,0,1:T(8,128)(2,1)S(1)} %get-tuple-element.8), kind=kOutput, calls=%fused_computation.22 | convolution fusion | flops 269484032 | bytes 2097152 | tf_op jit(solution)/shard_map/rck,ckn->rn/dot_general | solution.py:91
  202.9 1.6 constant_dynamic-slice_fusion.1
  204.5 22.5 %reduce-scatter.2.cloned.1.call-done = f32[256,128]{1,0:T(8,128)} async-done(((f32[256,512]{1,0:T(8,128)}), f32[256,128]{1,0:T(8,128)}) %reduce-scatter.2.cloned.1.call-update) | async-done | bytes 131088 | tf_op jit(solution)/shard_map/reduce_scatter | solution.py:94
  (68 shorter events, 1.5 us)
Async XLA Ops:
  7.2 119.7 %copy-start = (bf16[2,512,512]{2,1,0:T(8,128)(2,1)S(1)}, bf16[2,512,512]{2,1,0:T(8,128)(2,1)}, u32[]{:S(2)}) copy-start(bf16[2,512,512]{2,1,0:T(8,128)(2,1)} %param.20) | copy-start | bytes 3145732
  7.2 116.9 %all-gather.3.cloned.1.call-start = ((), (), s32[]{:S(2)}) async-start(), calls=%async_computation.2 | async-start | bytes 5242880 | tf_op jit(solution)/shard_map/all_gather | solution.py:82
  8.0 14.3 %copy-start.3 = (s32[8,512]{1,0:T(8,128)S(1)}, s32[8,512]{1,0:T(8,128)}, u32[]{:S(2)}) copy-start(s32[8,512]{1,0:T(8,128)} %param.25) | copy-start | bytes 49156
  8.0 15.5 %copy-start.7 = (s32[2,512]{1,0:T(2,128)S(1)}, s32[2,512]{1,0:T(2,128)}, u32[]{:S(2)}) copy-start(s32[2,512]{1,0:T(2,128)} %param.29) | copy-start | bytes 12292
  8.0 15.5 %copy-start.4 = (f32[8,512]{1,0:T(8,128)S(1)}, f32[8,512]{1,0:T(8,128)}, u32[]{:S(2)}) copy-start(f32[8,512]{1,0:T(8,128)} %param.26) | copy-start | bytes 49156
  13.2 14.0 %collective-permute-start = (bf16[256,2,512]{2,0,1:T(8,128)(2,1)S(1)}, bf16[256,2,512]{2,0,1:T(8,128)(2,1)S(1)}, u32[]{:S(2)}, u32[]{:S(2)}) collective-permute-start(bf16[256,2,512]{2,0,1:T(8,128)(2,1)S(1)} %pad_maximum_fusion.3), channel_id=1, source_target_pairs={{0,4},{4,8},{8,12},{12,16},{16,20},{20,24},{24,28},{28,32},{32,36}... | collective-permute-start | bytes 1572872 | tf_op jit(solution)/shard_map/ppermute | solution.py:14
  15.2 13.9 %collective-permute-start.1 = (bf16[256,2,512]{2,0,1:T(8,128)(2,1)S(1)}, bf16[256,2,512]{2,0,1:T(8,128)(2,1)}, u32[]{:S(2)}, u32[]{:S(2)}) collective-permute-start(bf16[256,2,512]{2,0,1:T(8,128)(2,1)S(1)} %pad_maximum_fusion.3), channel_id=1, source_target_pairs={{4,0},{8,4},{12,8},{16,12},{20,16},{24,20},{28,24},{32,28},{36,32}... | collective-permute-start | bytes 1572872 | tf_op jit(solution)/shard_map/ppermute | solution.py:15
  27.3 0.8 copy-start.2
  63.0 7.1 %copy-start.8 = (bf16[2,512,512]{2,1,0:T(8,128)(2,1)S(1)}, bf16[2,512,512]{2,1,0:T(8,128)(2,1)}, u32[]{:S(2)}) copy-start(bf16[2,512,512]{2,1,0:T(8,128)(2,1)} %param.19) | copy-start | bytes 3145732
  70.1 2.0 copy-start.5
  71.9 155.1 %reduce-scatter.2.cloned.1.call-start = ((), (), s32[]{:S(2)}) async-start(), calls=%async_computation.1 | async-start | bytes 655360 | tf_op jit(solution)/shard_map/reduce_scatter | solution.py:94
  126.9 5.4 %copy-start.1 = (bf16[512,512]{1,0:T(8,128)(2,1)}, bf16[512,512]{1,0:T(8,128)(2,1)S(1)}, u32[]{:S(2)}) copy-start(bf16[512,512]{1,0:T(8,128)(2,1)S(1)} %reduce_sum.9) | copy-start | bytes 1572868
  127.6 12.4 %copy-start.6 = (f32[8,256]{1,0:T(8,128)S(1)}, f32[8,256]{1,0:T(8,128)}, u32[]{:S(2)}) copy-start(f32[8,256]{1,0:T(8,128)} %param.28) | copy-start | bytes 24580
  132.3 18.2 %collective-permute-start.2 = (bf16[512,2,512]{0,2,1:T(8,128)(2,1)S(1)}, bf16[512,2,512]{0,2,1:T(8,128)(2,1)S(1)}, u32[]{:S(2)}, u32[]{:S(2)}) collective-permute-start(bf16[512,2,512]{0,2,1:T(8,128)(2,1)S(1)} %pad_maximum_fusion.2), channel_id=1, source_target_pairs={{0,4},{4,8},{8,12},{12,16},{16,20},{20,24},{24,28},{28,32},{32,36}... | collective-permute-start | bytes 3145736 | tf_op jit(solution)/shard_map/ppermute | solution.py:14
  134.2 18.1 %collective-permute-start.3 = (bf16[512,2,512]{0,2,1:T(8,128)(2,1)S(1)}, bf16[512,2,512]{0,2,1:T(8,128)(2,1)S(1)}, u32[]{:S(2)}, u32[]{:S(2)}) collective-permute-start(bf16[512,2,512]{0,2,1:T(8,128)(2,1)S(1)} %pad_maximum_fusion.2), channel_id=1, source_target_pairs={{4,0},{8,4},{12,8},{16,12},{20,16},{24,20},{28,24},{32,28},{36,32}... | collective-permute-start | bytes 3145736 | tf_op jit(solution)/shard_map/ppermute | solution.py:15
Sparse Core Ops, SparseCore 0:
  72.0 52.0 all-gather.2
  203.0 23.9 reduce-scatter.1
